TPU v7x, 256 devices: a whole 4x4x8 slice. The times are simulated.
256 devices in a mesh: outer: 8 (over z), inner: 32 (over x, y, core).
Axes of the slice: x: 4, y: 4, z: 8, core: 2. Of those that a mesh axis runs over, the one named last changes fastest.
Arguments:
- b_leaf: float32 [65536, 64], P(('outer', 'inner')), may hold values from -6 to 6
- b_sep: float32 [2048, 64], P(('outer', 'inner')), may hold values from -6 to 6
- b_root: float32 [2048, 64], P(('outer', 'inner')), may hold values from -6 to 6
- leaf_linv: float32 [65536, 256], P(('outer', 'inner')), as said below
- leaf_uinv: float32 [65536, 256], P(('outer', 'inner')), as said below
- leaf_lower: float32 [65536, 256], P(('outer', 'inner')), as said below
- leaf_upper: float32 [65536, 256], P(('outer', 'inner')), as said below
- sep_rows: int32 [256, 256], P(('outer', 'inner')), may hold values from 0 to 255, as said below
- sep_linv: float32 [2048, 256], P(('outer', 'inner')), as said below
- sep_uinv: float32 [2048, 256], P(('outer', 'inner')), as said below
- sep_lower: float32 [2048, 2048], P(None, ('outer', 'inner')), as said below
- sep_upper: float32 [2048, 2048], P(('outer', 'inner')), as said below
- root_linv: float32 [2048, 2048], P(('outer', 'inner')), as said below
- root_uinv: float32 [2048, 2048], P(('outer', 'inner')), as said below
- basis_leaf: float32 [65536, 512], P(('outer', 'inner')), as said below
- basis_sep: float32 [2048, 512], P(('outer', 'inner')), as said below
- basis_root: float32 [2048, 512], P(('outer', 'inner')), as said below
- g_blocks: float32 [262144, 128], P(('outer', 'inner')), may hold values from -0.25 to 0.25
- c_blocks: float32 [262144, 128], P(('outer', 'inner')), may hold values from -0.25 to 0.25
- block_cols: int32 [512, 4], P(('outer', 'inner')), may hold values from 0 to 1
Outputs:
- v_leaf: float32 [65536, 64], P(('outer', 'inner'))
- v_sep: float32 [2048, 64], P(('outer', 'inner'))
- v_root: float32 [2048, 64], P(('outer', 'inner'))
- coefficients: float32 [512, 64], replicated
- reduced_g: float32 [64, 64], replicated
- reduced_c: float32 [64, 64], replicated
Inputs may be any that keep to these rules, and one draw needn't show every extreme that they name: `sep_rows`: each row holds 256 distinct numbers; every row names 0 and 255. `leaf_linv`: lower triangular in each diagonal block of the stack, nonzero diagonal. `leaf_uinv`: upper triangular in each diagonal block of the stack, nonzero diagonal. `sep_linv`: lower triangular in each block of 256 rows, nonzero diagonal. `sep_uinv`: upper triangular in each block of 256 rows, nonzero diagonal. `root_linv`: lower triangular, nonzero diagonal. `root_uinv`: upper triangular, nonzero diagonal. `leaf_lower`: entries of order one over the square root of 256. `leaf_upper`: entries of order one over the square root of 256. `sep_lower`: entries of order one over the square root of the number of its columns. `sep_upper`: entries of order one over the square root of 2048. basis_leaf, basis_sep and basis_root stacked by rows form Q with Q^T Q = 69632 I up to float32 rounding. `basis_sep`: part of the stacked Q described with basis_leaf. `basis_root`: part of the stacked Q described with basis_leaf.
All inputs are finite; a program needn't handle non-finite values.
Results may differ from a plain program's by a relative error of at most 0.0003.
Values sent between devices are 32-bit elements; how exact they have to be, the bound alone decides.
A program may use at most 64 MiB of HBM per device.

v0:
```python
import jax
import jax.numpy as jnp
from jax import lax
from jax.sharding import PartitionSpec as P


def matmul_exact(left, right):
    return jnp.dot(left, right, precision=lax.Precision.HIGHEST, preferred_element_type=jnp.float32)


def contract_rows(left, right):
    return lax.dot_general(
        left,
        right,
        (((0,), (0,)), ((), ())),
        precision=lax.Precision.HIGHEST,
        preferred_element_type=jnp.float32,
    )


def shards(
    b_leaf,
    b_sep,
    b_root,
    leaf_linv,
    leaf_uinv,
    leaf_lower,
    leaf_upper,
    sep_rows,
    sep_linv,
    sep_uinv,
    sep_lower,
    sep_upper,
    root_linv,
    root_uinv,
    basis_leaf,
    basis_sep,
    basis_root,
    g_blocks,
    c_blocks,
    block_cols,
):
    ports = b_leaf.shape[1]
    sep_local = b_sep.shape[0]
    root_local = b_root.shape[0]
    sep_width = sep_linv.shape[1]
    selector = (sep_rows[0][:, None] == jnp.arange(sep_width, dtype=jnp.int32)[None, :]).astype(
        jnp.float32
    )
    y_leaf = matmul_exact(leaf_linv, b_leaf)
    contrib = matmul_exact(leaf_lower, y_leaf)
    t_sep = lax.psum_scatter(
        contract_rows(selector, contrib), "inner", scatter_dimension=0, tiled=True
    )
    sep_whole = lax.all_gather(b_sep - t_sep, "inner", axis=0, tiled=True)
    y_sep = matmul_exact(sep_linv, sep_whole)
    t_root = lax.psum_scatter(
        matmul_exact(sep_lower, y_sep), ("outer", "inner"), scatter_dimension=0, tiled=True
    )
    root_rhs = lax.all_gather(b_root - t_root, ("outer", "inner"), axis=0, tiled=True)
    y_root = matmul_exact(root_linv, root_rhs)
    y_root_all = lax.all_gather(y_root, ("outer", "inner"), axis=0, tiled=True)
    x_root = matmul_exact(root_uinv, y_root_all)
    x_root_all = lax.all_gather(x_root, ("outer", "inner"), axis=0, tiled=True)
    z_sep = y_sep - matmul_exact(sep_upper, x_root_all)
    z_sep_all = lax.all_gather(z_sep, "inner", axis=0, tiled=True)
    x_sep = matmul_exact(sep_uinv, z_sep_all)
    x_sep_all = lax.all_gather(x_sep, "inner", axis=0, tiled=True)
    coupled = matmul_exact(selector, x_sep_all)
    x_leaf = matmul_exact(leaf_uinv, y_leaf - matmul_exact(leaf_upper, coupled))
    node_count = float(
        lax.axis_size("outer") * lax.axis_size("inner") * (b_leaf.shape[0] + sep_local + root_local)
    )
    pieces_x = (x_leaf, x_sep, x_root)
    pieces_q = (basis_leaf, basis_sep, basis_root)
    projected = (
        contract_rows(basis_leaf, x_leaf)
        + contract_rows(basis_sep, x_sep)
        + contract_rows(basis_root, x_root)
    )
    coefficients = lax.psum(projected, ("outer", "inner")) / node_count
    cleaned = [
        values - matmul_exact(basis, coefficients) for basis, values in zip(pieces_q, pieces_x)
    ]
    local_gram = (
        contract_rows(cleaned[0], cleaned[0])
        + contract_rows(cleaned[1], cleaned[1])
        + contract_rows(cleaned[2], cleaned[2])
    )
    gram_matrix = lax.psum(local_gram, ("outer", "inner")) / node_count
    chol_lower = jnp.linalg.cholesky(gram_matrix)
    inverse_lower = lax.linalg.triangular_solve(
        chol_lower, jnp.eye(ports, dtype=jnp.float32), left_side=True, lower=True
    )
    v_leaf = matmul_exact(cleaned[0], inverse_lower.T)
    v_sep = matmul_exact(cleaned[1], inverse_lower.T)
    v_root = matmul_exact(cleaned[2], inverse_lower.T)
    block_rows = block_cols.shape[0]
    stored = block_cols.shape[1]
    block_size = g_blocks.shape[1]
    blocked = v_leaf.reshape(block_rows, block_size, ports)
    picked = blocked[block_cols]
    g_tiles = g_blocks.reshape(block_rows, stored, block_size, block_size)
    c_tiles = c_blocks.reshape(block_rows, stored, block_size, block_size)
    g_image = jnp.einsum("rwij,rwjp->rip", g_tiles, picked, precision=lax.Precision.HIGHEST)
    c_image = jnp.einsum("rwij,rwjp->rip", c_tiles, picked, precision=lax.Precision.HIGHEST)
    g_local = jnp.einsum("rip,riq->pq", blocked, g_image, precision=lax.Precision.HIGHEST)
    c_local = jnp.einsum("rip,riq->pq", blocked, c_image, precision=lax.Precision.HIGHEST)
    g_summed, c_summed = lax.psum((g_local, c_local), ("outer", "inner"))
    return (v_leaf, v_sep, v_root, coefficients, g_summed / node_count, c_summed / node_count)


def solution(mesh):
    return jax.shard_map(
        shards,
        mesh=mesh,
        in_specs=(
            P(("outer", "inner"), None),
            P(("outer", "inner"), None),
            P(("outer", "inner"), None),
            P(("outer", "inner"), None),
            P(("outer", "inner"), None),
            P(("outer", "inner"), None),
            P(("outer", "inner"), None),
            P(("outer", "inner"), None),
            P(("outer", "inner"), None),
            P(("outer", "inner"), None),
            P(None, ("outer", "inner")),
            P(("outer", "inner"), None),
            P(("outer", "inner"), None),
            P(("outer", "inner"), None),
            P(("outer", "inner"), None),
            P(("outer", "inner"), None),
            P(("outer", "inner"), None),
            P(("outer", "inner"), None),
            P(("outer", "inner"), None),
            P(("outer", "inner"), None),
        ),
        out_specs=(
            P(("outer", "inner"), None),
            P(("outer", "inner"), None),
            P(("outer", "inner"), None),
            P(),
            P(),
            P(),
        ),
        check_vma=False,
    )
```

profile of v0, /device:TPU:1, one launch (start us, length us, event | category | flops | bytes accessed | tf_op | source)
XLA Modules:
  0.0 1057.3 jit_solution(8577901284034292284)
XLA Ops:
  7.2 1.4 fusion.16
  8.6 0.4 fusion.17
  9.0 0.7 copy-done.16
  9.7 1.0 fusion.8
  10.8 0.7 copy-done.20
  11.5 0.6 dynamic-slice
  12.7 112.8 %all-reduce.9.cloned.1.call-done = f32[256,64]{1,0:T(8,128)} async-done(((f32[256,64]{1,0:T(8,128)}), f32[256,64]{1,0:T(8,128)}) %all-reduce.9.cloned.1.call-update) | async-done | bytes 65552
  125.5 0.7 dynamic-slice_subtract_fusion.1
  126.2 25.7 %all_gather.18 = f32[256,64]{1,0:T(8,128)S(1)} all-gather(f32[8,64]{1,0:T(8,128)S(1)} %dynamic-slice_subtract_fusion.1), channel_id=1, replica_groups=mesh['outer'=8,'inner'=32] {'inner'}, dimensions={0}, use_global_device_ids=true | all-gather | bytes 67584 | tf_op jit(solution)/shard_map/all_gather | solution.py:55
  152.0 0.7 copy-done.8
  152.7 0.6 convolution_bitcast_fusion
  153.3 1.3 copy.47
  154.8 0.6 copy-done.19
  155.4 251.8 %all-reduce.11.cloned.1.call-done = f32[2048,64]{1,0:T(8,128)} async-done(((f32[2048,64]{1,0:T(8,128)}), f32[2048,64]{1,0:T(8,128)}) %all-reduce.11.cloned.1.call-update) | async-done | bytes 524304
  407.2 0.7 dynamic-slice_subtract_fusion
  407.9 63.2 %all_gather.19 = f32[2048,64]{1,0:T(8,128)S(1)} all-gather(f32[8,64]{1,0:T(8,128)S(1)} %dynamic-slice_subtract_fusion), channel_id=1, replica_groups=mesh['outer'=8,'inner'=32] {'outer','inner'}, dimensions={0}, use_global_device_ids=true | all-gather | bytes 526336 | tf_op jit(solution)/shard_map/all_gather | solution.py:60
  471.1 0.7 convolution_bitcast_fusion.8
  471.7 60.2 %all_gather.20 = f32[2048,64]{1,0:T(8,128)S(1)} all-gather(f32[8,64]{1,0:T(8,128)S(1)} %convolution_bitcast_fusion.8), channel_id=1, replica_groups=mesh['outer'=8,'inner'=32] {'outer','inner'}, dimensions={0}, use_global_device_ids=true | all-gather | bytes 526336 | tf_op jit(solution)/shard_map/all_gather | solution.py:62
  532.0 0.7 fusion.19
  532.6 60.4 %all_gather.21 = f32[2048,64]{1,0:T(8,128)S(1)} all-gather(f32[8,64]{1,0:T(8,128)S(1)} %bitcast.121), channel_id=1, replica_groups=mesh['outer'=8,'inner'=32] {'outer','inner'}, dimensions={0}, use_global_device_ids=true | all-gather | bytes 526336 | tf_op jit(solution)/shard_map/all_gather | solution.py:64
  593.1 0.7 fusion.5
  593.7 23.3 %all_gather.22 = f32[256,64]{1,0:T(8,128)S(1)} all-gather(f32[8,64]{1,0:T(8,128)S(1)} %fusion.5), channel_id=1, replica_groups=mesh['outer'=8,'inner'=32] {'inner'}, dimensions={0}, use_global_device_ids=true | all-gather | bytes 67584 | tf_op jit(solution)/shard_map/all_gather | solution.py:66
  617.2 23.0 %all_gather.23 = f32[256,64]{1,0:T(8,128)S(1)} all-gather(f32[8,64]{1,0:T(8,128)S(1)} %bitcast.122), channel_id=1, replica_groups=mesh['outer'=8,'inner'=32] {'inner'}, dimensions={0}, use_global_device_ids=true | all-gather | bytes 67584 | tf_op jit(solution)/shard_map/all_gather | solution.py:68
  640.2 0.3 fusion.6
  640.6 0.3 fusion.22
  640.9 0.3 fusion.23
  641.3 0.4 fusion.2
  641.6 0.4 fusion.21
  642.0 1.1 fusion.1
  643.1 237.7 %all-reduce.7.cloned.1.call-done = f32[512,64]{0,1:T(8,128)} async-done(((f32[512,64]{0,1:T(8,128)}), f32[512,64]{0,1:T(8,128)}) %all-reduce.7.cloned.1.call-update) | async-done | bytes 131088 | tf_op jit(solution)/shard_map/psum | solution.py:81
  880.8 0.9 broadcast_multiply_fusion
  881.8 0.6 convolution_subtract_fusion
  882.8 0.2 fusion.24
  883.0 0.2 convolution_add_fusion.2
  883.3 0.2 convolution_add_fusion.1
  883.5 76.0 %psum.29 = f32[64,64]{0,1:T(8,128)S(1)} all-reduce(f32[64,64]{0,1:T(8,128)S(1)} %convolution_add_fusion.1), channel_id=1, replica_groups=mesh['outer'=8,'inner'=32] {'outer','inner'}, use_global_device_ids=true, to_apply=%region_3.0 | all-reduce | flops 4096 | bytes 32768 | tf_op jit(solution)/shard_map/psum | solution.py:90
  959.7 5.8 cholesky.17
  965.6 0.6 compare_reduce_fusion
  966.2 0.7 fusion.12
  966.9 4.9 custom-call.6
  972.2 0.8 fusion.27
  973.0 0.8 fusion.26
  973.7 0.6 gather_fusion
  974.3 0.7 convolution_bitcast_fusion.1
  975.4 0.7 convolution_bitcast_fusion.2
  976.2 73.1 %all-reduce.2 = (f32[64,64]{0,1:T(8,128)S(1)}, f32[64,64]{0,1:T(8,128)S(1)}) all-reduce(f32[64,64]{0,1:T(8,128)S(1)} %convolution_bitcast_fusion.5, f32[64,64]{0,1:T(8,128)S(1)} %convolution_bitcast_fusion.4), channel_id=1, replica_groups=mesh['outer'=8,'inner'=32] {'outer','inner'}, use_global_device_ids=true, to_apply=%region_6.7 | all-reduce | flops 8192 | bytes 65536 | tf_op jit(solution)/shard_map/psum | solution.py:109
  1049.4 0.7 copy.57
  1050.1 0.7 copy.58
  (61 shorter events, 2.3 us)
Async XLA Ops:
  7.2 967.2 %copy-start = (f32[1024,128]{1,0:T(8,128)S(1)}, f32[1024,128]{1,0:T(8,128)}, u32[]{:S(2)}) copy-start(f32[1024,128]{1,0:T(8,128)} %param.38) | copy-start | bytes 1572868
  7.2 1.5 copy-start.6
  7.2 118.3 %all-reduce.9.cloned.1.call-start = ((), (), s32[]{:S(2)}) async-start(), calls=%async_computation.1 | async-start | bytes 262144
  9.0 0.7 copy-start.16
  10.8 396.5 %all-reduce.11.cloned.1.call-start = ((), (), s32[]{:S(2)}) async-start(), calls=%async_computation.2 | async-start | bytes 2097152
  10.8 0.7 copy-start.20
  11.5 114.0 %copy-start.17 = (f32[8,64]{1,0:T(8,128)S(1)}, f32[8,64]{1,0:T(8,128)}, u32[]{:S(2)}) copy-start(f32[8,64]{1,0:T(8,128)} %param.21) | copy-start | bytes 6148
  126.2 25.7 %copy-start.14 = (f32[8,256]{1,0:T(8,128)S(1)}, f32[8,256]{1,0:T(8,128)}, u32[]{:S(2)}) copy-start(f32[8,256]{1,0:T(8,128)} %param.28) | copy-start | bytes 24580
  151.8 0.8 copy-start.8
  154.7 0.7 copy-start.19
  154.7 252.5 %copy-start.18 = (f32[8,64]{1,0:T(8,128)S(1)}, f32[8,64]{1,0:T(8,128)}, u32[]{:S(2)}) copy-start(f32[8,64]{1,0:T(8,128)} %param.22) | copy-start | bytes 6148
  154.7 726.1 %all-reduce.7.cloned.1.call-start = ((), (), s32[]{:S(2)}) async-start(), calls=%async_computation | async-start | bytes 262144 | tf_op jit(solution)/shard_map/psum | solution.py:81
  407.9 63.2 %copy-start.9 = (f32[8,2048]{1,0:T(8,128)S(1)}, f32[8,2048]{1,0:T(8,128)}, u32[]{:S(2)}) copy-start(f32[8,2048]{1,0:T(8,128)} %param.32) | copy-start | bytes 196612
  471.7 60.2 %copy-start.10 = (f32[8,2048]{1,0:T(8,128)S(1)}, f32[8,2048]{1,0:T(8,128)}, u32[]{:S(2)}) copy-start(f32[8,2048]{1,0:T(8,128)} %param.33) | copy-start | bytes 196612
  532.6 60.4 %copy-start.11 = (f32[8,2048]{1,0:T(8,128)S(1)}, f32[8,2048]{1,0:T(8,128)}, u32[]{:S(2)}) copy-start(f32[8,2048]{1,0:T(8,128)} %param.31) | copy-start | bytes 196612
  593.7 23.3 %copy-start.15 = (f32[8,256]{1,0:T(8,128)S(1)}, f32[8,256]{1,0:T(8,128)}, u32[]{:S(2)}) copy-start(f32[8,256]{1,0:T(8,128)} %param.29) | copy-start | bytes 24580
  617.2 23.4 %copy-start.12 = (f32[8,512]{1,0:T(8,128)S(1)}, f32[8,512]{1,0:T(8,128)}, u32[]{:S(2)}) copy-start(f32[8,512]{1,0:T(8,128)} %param.35) | copy-start | bytes 49156
  640.2 0.7 copy-start.13
  640.2 1.0 copy-start.5
  640.6 1.1 copy-start.7
  640.9 1.1 copy-start.1
  881.8 0.8 copy-start.2
  972.2 3.8 copy-start.3
  974.3 1.0 copy-start.4
Sparse Core Ops, SparseCore 0:
  11.8 113.6 all-reduce.8
  154.8 252.3 all-reduce.10
  643.3 237.5 all-reduce.6
where the time goes:
time: 1060 us
  waiting for transfers between devices  602 us (57%)
  blocking collectives  405 us (38%)
  between operations  14.7 us (1%)
  other arithmetic  14.4 us (1%)
  matrix products  14 us (1%)
    unnamed x5, waiting for transfers between devices  365 us
    psum x1, waiting for transfers between devices, shards(): coefficients = lax.psum(projected, ('outer', 'inner')) / node_count  238 us
    psum x1, blocking collectives, shards(): gram_matrix = lax.psum(local_gram, ('outer', 'inner')) / node_count  76 us
    psum x1, blocking collectives, shards(): g_summed, c_summed = lax.psum((g_local, c_local), ('outer', 'inner'))  73.1 us
    all_gather x1, blocking collectives, shards(): lax.all_gather(b_root - t_root, ('outer', 'inner'), axis=0, tiled=True)  63.2 us
    all_gather x1, blocking collectives, shards(): x_root_all = lax.all_gather(x_root, ('outer', 'inner'), axis=0, tiled=True)  60.4 us
    all_gather x1, blocking collectives, shards(): y_root_all = lax.all_gather(y_root, ('outer', 'inner'), axis=0, tiled=True)  60.2 us
    all_gather x1, blocking collectives, shards(): sep_whole = lax.all_gather(b_sep - t_sep, 'inner', axis=0, tiled=True)  25.7 us
  transfers between devices with their start and end apart: 3, of which 3 were waited for; matrix products, arithmetic and copies ran while one was open for 0% of the time, Pallas kernels for 0%

commit v1 on v0

--- a/solution.py
+++ b/solution.py
@@ -63,7 +63,9 @@
     x_root = matmul_exact(root_uinv, y_root_all)
     x_root_all = lax.all_gather(x_root, ("outer", "inner"), axis=0, tiled=True)
     z_sep = y_sep - matmul_exact(sep_upper, x_root_all)
-    z_sep_all = lax.all_gather(z_sep, "inner", axis=0, tiled=True)
+    z_sep_all = jnp.concatenate(
+        lax.all_to_all(jnp.stack([z_sep] * lax.axis_size("inner")), "inner", 0, 0), axis=0
+    )
     x_sep = matmul_exact(sep_uinv, z_sep_all)
     x_sep_all = lax.all_gather(x_sep, "inner", axis=0, tiled=True)
     coupled = matmul_exact(selector, x_sep_all)

time: 1060 us -> 1050 us (level)
  blocking collectives: 405 us -> 382 us
    all_gather x1 -> x0, blocking collectives: 23.3 us -> none  [shards(): z_sep_all = lax.all_gather(z_sep, 'inner', axis=0, tiled=True)]
  transfers between devices with their start and end apart: 3 -> 4, of which waited for: 3 -> 4; matrix products, arithmetic and copies ran while one was open for 0% -> 0% of each run, Pallas kernels for 0% -> 0%
where the time goes in v1:
time: 1050 us
  waiting for transfers between devices  609 us (58%)
  blocking collectives  382 us (36%)
  other arithmetic  15.2 us (1%)
  between operations  14.8 us (1%)
  matrix products  14 us (1%)
    unnamed x5, waiting for transfers between devices  365 us
    psum x1, waiting for transfers between devices, shards(): coefficients = lax.psum(projected, ('outer', 'inner')) / node_count  238 us
    psum x1, blocking collectives, shards(): gram_matrix = lax.psum(local_gram, ('outer', 'inner')) / node_count  76 us
    psum x1, blocking collectives, shards(): g_summed, c_summed = lax.psum((g_local, c_local), ('outer', 'inner'))  73.1 us
    all_gather x1, blocking collectives, shards(): lax.all_gather(b_root - t_root, ('outer', 'inner'), axis=0, tiled=True)  63.1 us
    all_gather x1, blocking collectives, shards(): x_root_all = lax.all_gather(x_root, ('outer', 'inner'), axis=0, tiled=True)  60.4 us
    all_gather x1, blocking collectives, shards(): y_root_all = lax.all_gather(y_root, ('outer', 'inner'), axis=0, tiled=True)  60.2 us
    all_gather x1, blocking collectives, shards(): sep_whole = lax.all_gather(b_sep - t_sep, 'inner', axis=0, tiled=True)  25.7 us
  transfers between devices with their start and end apart: 4, of which 4 were waited for; matrix products, arithmetic and copies ran while one was open for 0% of the time, Pallas kernels for 0%

profile of v1, /device:TPU:1, one launch (start us, length us, event | category | flops | bytes accessed | tf_op | source)
XLA Modules:
  0.0 1048.3 jit_solution(3166842034302406417)
XLA Ops:
  7.2 1.4 fusion.18
  8.6 0.4 fusion.19
  9.0 0.7 copy-done.16
  9.7 1.0 fusion.8
  10.8 0.7 copy-done.20
  11.5 0.6 dynamic-slice
  12.7 112.8 %all-reduce.9.cloned.1.call-done = f32[256,64]{1,0:T(8,128)} async-done(((f32[256,64]{1,0:T(8,128)}), f32[256,64]{1,0:T(8,128)}) %all-reduce.9.cloned.1.call-update) | async-done | bytes 65552
  125.5 0.7 dynamic-slice_subtract_fusion.1
  126.2 25.7 %all_gather.15 = f32[256,64]{1,0:T(8,128)S(1)} all-gather(f32[8,64]{1,0:T(8,128)S(1)} %dynamic-slice_subtract_fusion.1), channel_id=1, replica_groups=mesh['outer'=8,'inner'=32] {'inner'}, dimensions={0}, use_global_device_ids=true | all-gather | bytes 67584 | tf_op jit(solution)/shard_map/all_gather | solution.py:55
  152.0 0.7 copy-done.8
  152.7 0.6 convolution_bitcast_fusion
  153.3 1.4 copy.47
  154.7 0.7 copy-done.19
  155.5 251.8 %all-reduce.11.cloned.1.call-done = f32[2048,64]{1,0:T(8,128)} async-done(((f32[2048,64]{1,0:T(8,128)}), f32[2048,64]{1,0:T(8,128)}) %all-reduce.11.cloned.1.call-update) | async-done | bytes 524304
  407.2 0.7 dynamic-slice_subtract_fusion
  407.9 63.1 %all_gather.16 = f32[2048,64]{1,0:T(8,128)S(1)} all-gather(f32[8,64]{1,0:T(8,128)S(1)} %dynamic-slice_subtract_fusion), channel_id=1, replica_groups=mesh['outer'=8,'inner'=32] {'outer','inner'}, dimensions={0}, use_global_device_ids=true | all-gather | bytes 526336 | tf_op jit(solution)/shard_map/all_gather | solution.py:60
  471.1 0.7 convolution_bitcast_fusion.8
  471.7 60.2 %all_gather.17 = f32[2048,64]{1,0:T(8,128)S(1)} all-gather(f32[8,64]{1,0:T(8,128)S(1)} %convolution_bitcast_fusion.8), channel_id=1, replica_groups=mesh['outer'=8,'inner'=32] {'outer','inner'}, dimensions={0}, use_global_device_ids=true | all-gather | bytes 526336 | tf_op jit(solution)/shard_map/all_gather | solution.py:62
  531.9 0.7 fusion.21
  532.6 60.4 %all_gather.18 = f32[2048,64]{1,0:T(8,128)S(1)} all-gather(f32[8,64]{1,0:T(8,128)S(1)} %bitcast.123), channel_id=1, replica_groups=mesh['outer'=8,'inner'=32] {'outer','inner'}, dimensions={0}, use_global_device_ids=true | all-gather | bytes 526336 | tf_op jit(solution)/shard_map/all_gather | solution.py:64
  593.0 0.7 fusion.5
  593.7 0.8 reshape.55
  594.5 4.4 all-to-all-start
  599.2 7.0 all-to-all-done
  606.2 0.5 broadcast.76
  606.7 0.8 reduce.6
  607.6 0.6 copy-done.15
  608.4 23.1 %all_gather.19 = f32[256,64]{1,0:T(8,128)S(1)} all-gather(f32[8,64]{1,0:T(8,128)S(1)} %bitcast.124), channel_id=1, replica_groups=mesh['outer'=8,'inner'=32] {'inner'}, dimensions={0}, use_global_device_ids=true | all-gather | bytes 67584 | tf_op jit(solution)/shard_map/all_gather | solution.py:70
  631.5 0.3 fusion.6
  632.2 0.4 fusion.2
  632.6 0.4 fusion.22
  633.0 1.1 fusion.1
  634.1 237.7 %all-reduce.7.cloned.1.call-done = f32[512,64]{0,1:T(8,128)} async-done(((f32[512,64]{0,1:T(8,128)}), f32[512,64]{0,1:T(8,128)}) %all-reduce.7.cloned.1.call-update) | async-done | bytes 131088 | tf_op jit(solution)/shard_map/psum | solution.py:83
  871.9 0.9 broadcast_multiply_fusion
  872.8 0.6 convolution_subtract_fusion
  874.6 76.0 %psum.29 = f32[64,64]{0,1:T(8,128)S(1)} all-reduce(f32[64,64]{0,1:T(8,128)S(1)} %convolution_add_fusion.1), channel_id=1, replica_groups=mesh['outer'=8,'inner'=32] {'outer','inner'}, use_global_device_ids=true, to_apply=%region_3.0 | all-reduce | flops 4096 | bytes 32768 | tf_op jit(solution)/shard_map/psum | solution.py:92
  950.7 5.8 cholesky.17
  956.6 0.6 compare_reduce_fusion
  957.2 0.7 fusion.14
  957.9 4.9 custom-call.6
  963.2 0.8 fusion.28
  964.0 0.8 fusion.27
  964.8 0.6 gather_fusion
  965.4 0.7 convolution_bitcast_fusion.1
  966.4 0.7 convolution_bitcast_fusion.2
  967.3 73.1 %all-reduce.2 = (f32[64,64]{0,1:T(8,128)S(1)}, f32[64,64]{0,1:T(8,128)S(1)}) all-reduce(f32[64,64]{0,1:T(8,128)S(1)} %convolution_bitcast_fusion.5, f32[64,64]{0,1:T(8,128)S(1)} %convolution_bitcast_fusion.4), channel_id=1, replica_groups=mesh['outer'=8,'inner'=32] {'outer','inner'}, use_global_device_ids=true, to_apply=%region_6.7 | all-reduce | flops 8192 | bytes 65536 | tf_op jit(solution)/shard_map/psum | solution.py:111
  1040.4 0.7 copy.57
  1041.1 0.7 copy.58
  (67 shorter events, 3.7 us)
Async XLA Ops:
  7.2 958.2 %copy-start = (f32[1024,128]{1,0:T(8,128)S(1)}, f32[1024,128]{1,0:T(8,128)}, u32[]{:S(2)}) copy-start(f32[1024,128]{1,0:T(8,128)} %param.38) | copy-start | bytes 1572868
  7.2 1.5 copy-start.6
  7.2 118.3 %all-reduce.9.cloned.1.call-start = ((), (), s32[]{:S(2)}) async-start(), calls=%async_computation.2 | async-start | bytes 262144
  9.0 0.7 copy-start.16
  10.8 396.4 %all-reduce.11.cloned.1.call-start = ((), (), s32[]{:S(2)}) async-start(), calls=%async_computation.3 | async-start | bytes 2097152
  10.8 0.7 copy-start.20
  11.5 114.0 %copy-start.17 = (f32[8,64]{1,0:T(8,128)S(1)}, f32[8,64]{1,0:T(8,128)}, u32[]{:S(2)}) copy-start(f32[8,64]{1,0:T(8,128)} %param.21) | copy-start | bytes 6148
  126.2 25.7 %copy-start.14 = (f32[8,256]{1,0:T(8,128)S(1)}, f32[8,256]{1,0:T(8,128)}, u32[]{:S(2)}) copy-start(f32[8,256]{1,0:T(8,128)} %param.28) | copy-start | bytes 24580
  151.8 0.8 copy-start.8
  154.7 0.7 copy-start.19
  154.7 252.5 %copy-start.18 = (f32[8,64]{1,0:T(8,128)S(1)}, f32[8,64]{1,0:T(8,128)}, u32[]{:S(2)}) copy-start(f32[8,64]{1,0:T(8,128)} %param.22) | copy-start | bytes 6148
  407.9 63.2 %copy-start.9 = (f32[8,2048]{1,0:T(8,128)S(1)}, f32[8,2048]{1,0:T(8,128)}, u32[]{:S(2)}) copy-start(f32[8,2048]{1,0:T(8,128)} %param.32) | copy-start | bytes 196612
  471.7 60.2 %copy-start.10 = (f32[8,2048]{1,0:T(8,128)S(1)}, f32[8,2048]{1,0:T(8,128)}, u32[]{:S(2)}) copy-start(f32[8,2048]{1,0:T(8,128)} %param.33) | copy-start | bytes 196612
  532.6 60.4 %copy-start.11 = (f32[8,2048]{1,0:T(8,128)S(1)}, f32[8,2048]{1,0:T(8,128)}, u32[]{:S(2)}) copy-start(f32[8,2048]{1,0:T(8,128)} %param.31) | copy-start | bytes 196612
  594.5 4.4 copy-start.13
  594.5 11.7 %all-to-all-start = ((f32[32,1,512]{2,1,0:T(1,128)}), f32[32,1,512]{2,1,0:T(1,128)S(1)}, u32[]{:S(2)}, u32[]{:S(2)}) async-start(f32[32,1,512]{2,1,0:T(1,128)} %reshape.55), calls=%async_computation | async-start | bytes 131072 | tf_op jit(solution)/shard_map/all_to_all | solution.py:67
  598.9 273.0 %all-reduce.7.cloned.1.call-start = ((), (), s32[]{:S(2)}) async-start(), calls=%async_computation.1 | async-start | bytes 262144 | tf_op jit(solution)/shard_map/psum | solution.py:83
  607.6 0.7 copy-start.15
  608.4 23.8 %copy-start.5 = (f32[256,256]{1,0:T(8,128)S(1)}, f32[256,256]{1,0:T(8,128)}, u32[]{:S(2)}) copy-start(f32[256,256]{1,0:T(8,128)} %param.26) | copy-start | bytes 786436
  608.4 23.4 %copy-start.12 = (f32[8,512]{1,0:T(8,128)S(1)}, f32[8,512]{1,0:T(8,128)}, u32[]{:S(2)}) copy-start(f32[8,512]{1,0:T(8,128)} %param.35) | copy-start | bytes 49156
  631.5 1.1 copy-start.7
  631.9 1.1 copy-start.1
  872.8 0.8 copy-start.2
  963.2 3.8 copy-start.3
  965.3 1.0 copy-start.4
Sparse Core Ops, SparseCore 0:
  11.8 113.6 all-reduce.8
  154.8 252.3 all-reduce.10
  634.2 237.5 all-reduce.6
